TPU v7x, 32 devices: a whole 2x2x4 slice. The times are simulated.
32 devices in a mesh: seq: 4 (over y, x), tp: 8 (over z, core).
Axes of the slice: x: 2, y: 2, z: 4, core: 2. Of those that a mesh axis runs over, the one named last changes fastest.
Arguments:
- hidden_in: bfloat16 [1024, 5120], P('seq', 'tp'), may hold values from -16 to 16
- seg_ids: int32 [1024], P('seq'), may hold values from 0 to 3, never falling along the last dimension, each value on 1 to 640 neighbouring positions
- positions: int32 [3, 1024], P(None, 'seq'), may hold values from 0 to 63
- mod_table: float32 [4, 3, 5120], P(None, None, 'tp'), may hold values from -4 to 4
- w_qkv: bfloat16 [5120, 3, 4096], P('seq', None, 'tp')
- q_gain: float32 [4096], P('tp'), may hold values from 0.5 to 3.5
- k_gain: float32 [4096], P('tp'), may hold values from 0.5 to 3.5
- w_out: bfloat16 [4096, 5120], P('tp', 'seq'), may hold values from -0.125 to 0.125
Outputs:
- hidden_out: bfloat16 [1024, 5120], P('seq', 'tp')
- k_cache: bfloat16 [1024, 4096], P('seq', 'tp')
- v_cache: bfloat16 [1024, 4096], P('seq', 'tp')
Inputs may be any that keep to these rules, and one draw needn't show every extreme that they name: `seg_ids`: segment ids never fall along the stream; each segment holds 1 to 640 tokens, and one holds exactly 640.
All inputs are finite; a program needn't handle non-finite values.
Results may differ from a plain program's by a relative error of at most 0.018.
Values may be sent and summed in bfloat16 or wider, within the bound.
A program may use at most 64 MiB of HBM per device.

v0:
```python
import math

import jax
import jax.numpy as jnp
from jax import lax
from jax.sharding import PartitionSpec as P

HEAD_DIM = 128


EPSILON = 1e-06
NEG_FILL = -1e30


def rope_tables(positions):
    part_width = HEAD_DIM // 6
    widths = (HEAD_DIM - 4 * part_width, 2 * part_width, 2 * part_width)
    angle_list = []
    for axis_number in range(3):
        exponent = jnp.arange(0, widths[axis_number], 2, dtype=jnp.float32) / widths[axis_number]
        frequency = 1.0 / 10000.0**exponent
        angle_list.append(positions[axis_number].astype(jnp.float32)[:, None] * frequency[None, :])
    angle_all = jnp.concatenate(angle_list, axis=1)
    return (jnp.cos(angle_all), jnp.sin(angle_all))


def rotate_pairs(field, cosine, sine):
    even_part = field[..., 0::2]
    odd_part = field[..., 1::2]
    cos_wide = cosine[:, None, :]
    sin_wide = sine[:, None, :]
    new_even = even_part * cos_wide - odd_part * sin_wide
    new_odd = even_part * sin_wide + odd_part * cos_wide
    return jnp.stack([new_even, new_odd], axis=-1).reshape(field.shape)


def empty_state(query_rows, heads_here):
    maxima = jnp.full((heads_here, query_rows), NEG_FILL, jnp.float32)
    totals = jnp.zeros((heads_here, query_rows), jnp.float32)
    weighted = jnp.zeros((heads_here, query_rows, HEAD_DIM), jnp.float32)
    return (maxima, totals, weighted)


def merge_states(first, second):
    largest = jnp.maximum(first[0], second[0])
    first_factor = jnp.exp(first[0] - largest)
    second_factor = jnp.exp(second[0] - largest)
    totals = first[1] * first_factor + second[1] * second_factor
    weighted = first[2] * first_factor[..., None] + second[2] * second_factor[..., None]
    return (largest, totals, weighted)


def block_state(q_heads, seg_q, key_heads, value_heads, seg_k):
    score_scale = 1.0 / math.sqrt(HEAD_DIM)
    scores = (
        jnp.einsum("qhd,khd->hqk", q_heads, key_heads, preferred_element_type=jnp.float32)
        * score_scale
    )
    same_seg = seg_q[:, None] == seg_k[None, :]
    masked = jnp.where(same_seg[None], scores, NEG_FILL)
    maxima = jnp.max(masked, axis=2)
    weights = jnp.where(same_seg[None], jnp.exp(masked - maxima[..., None]), 0.0)
    totals = jnp.sum(weights, axis=2)
    weighted = jnp.einsum(
        "hqk,khd->hqd",
        weights.astype(jnp.bfloat16),
        value_heads,
        preferred_element_type=jnp.float32,
    )
    return (maxima, totals, weighted)


def absorb_keys(carry_state, q_heads, seg_q, key_rows, value_rows, seg_k):
    row_count = key_rows.shape[0]
    heads_here = q_heads.shape[1]
    block_rows = 512
    block_count = row_count // block_rows
    key_blocks = key_rows.reshape(block_count, block_rows, heads_here, HEAD_DIM)
    value_blocks = value_rows.reshape(block_count, block_rows, heads_here, HEAD_DIM)
    seg_blocks = seg_k.reshape(block_count, block_rows)

    def step_block(state_now, operands):
        key_block, value_block, seg_block = operands
        return (
            merge_states(state_now, block_state(q_heads, seg_q, key_block, value_block, seg_block)),
            None,
        )

    return lax.scan(step_block, carry_state, (key_blocks, value_blocks, seg_blocks))[0]


def body(hidden_in, seg_ids, positions, mod_table, w_qkv, q_gain, k_gain, w_out):
    tok_rows, feat_local = hidden_in.shape
    model_width = feat_local * lax.axis_size("tp")
    heads_width = w_qkv.shape[2]
    heads_here = heads_width // HEAD_DIM
    all_heads_width = heads_width * lax.axis_size("tp")
    x_float = hidden_in.astype(jnp.float32)
    row_sums, row_squares = lax.psum(
        (jnp.sum(x_float, axis=1), jnp.sum(x_float * x_float, axis=1)), "tp"
    )
    mean_value = row_sums / model_width
    variance = row_squares / model_width - mean_value * mean_value
    normed = (x_float - mean_value[:, None]) * lax.rsqrt(variance[:, None] + EPSILON)
    segment_count = mod_table.shape[0]
    table = mod_table.reshape(segment_count, 3 * feat_local)
    onehot = (seg_ids[:, None] == jnp.arange(segment_count, dtype=jnp.int32)[None, :]).astype(
        jnp.float32
    )
    modulation = jnp.dot(onehot, table, precision=lax.Precision.HIGHEST).reshape(
        tok_rows, 3, feat_local
    )
    modded = (normed * (1.0 + modulation[:, 1]) + modulation[:, 0]).astype(jnp.bfloat16)
    full_rows = lax.all_gather(modded, "tp", axis=1, tiled=True)
    portion = lax.all_gather(w_qkv, "seq", axis=0, tiled=True)
    flat = portion.reshape(portion.shape[0], 3 * heads_width)
    projected = jnp.dot(full_rows, flat, preferred_element_type=jnp.float32)
    query_f = projected[:, :heads_width]
    key_f = projected[:, heads_width : 2 * heads_width]
    value_f = projected[:, 2 * heads_width :]
    query_sq, key_sq = lax.psum(
        (jnp.sum(query_f * query_f, axis=1), jnp.sum(key_f * key_f, axis=1)), "tp"
    )
    query_n = query_f * lax.rsqrt(query_sq / all_heads_width + EPSILON)[:, None] * q_gain[None, :]
    key_n = key_f * lax.rsqrt(key_sq / all_heads_width + EPSILON)[:, None] * k_gain[None, :]
    cosine, sine = rope_tables(positions)
    q_heads = rotate_pairs(query_n.reshape(tok_rows, heads_here, HEAD_DIM), cosine, sine).astype(
        jnp.bfloat16
    )
    k_heads = rotate_pairs(key_n.reshape(tok_rows, heads_here, HEAD_DIM), cosine, sine).astype(
        jnp.bfloat16
    )
    k_cache = k_heads.reshape(tok_rows, heads_width)
    v_cache = value_f.astype(jnp.bfloat16)
    key_rows = lax.all_gather(k_cache, "seq", axis=0, tiled=True)
    value_rows = lax.all_gather(v_cache, "seq", axis=0, tiled=True)
    seg_k = lax.all_gather(seg_ids, "seq", axis=0, tiled=True)
    state_end = absorb_keys(
        empty_state(tok_rows, heads_here), q_heads, seg_ids, key_rows, value_rows, seg_k
    )
    attention = (state_end[2] / state_end[1][..., None]).transpose(1, 0, 2)
    attn_out = attention.reshape(tok_rows, heads_width).astype(jnp.bfloat16)
    terms = jnp.dot(
        attn_out,
        lax.all_gather(w_out, "seq", axis=1, tiled=True),
        preferred_element_type=jnp.float32,
    )
    mixed = lax.psum_scatter(
        terms.astype(jnp.bfloat16), "tp", scatter_dimension=1, tiled=True
    ).astype(jnp.float32)
    hidden_out = (x_float + modulation[:, 2] * mixed).astype(jnp.bfloat16)
    return (hidden_out, k_cache, v_cache)


def solution(mesh):
    in_specs = (
        P("seq", "tp"),
        P("seq"),
        P(None, "seq"),
        P(None, None, "tp"),
        P("seq", None, "tp"),
        P("tp"),
        P("tp"),
        P("tp", "seq"),
    )
    out_specs = (P("seq", "tp"), P("seq", "tp"), P("seq", "tp"))
    return jax.shard_map(body, mesh=mesh, in_specs=in_specs, out_specs=out_specs, check_vma=False)
```

profile of v0, /device:TPU:14, one launch (start us, length us, event | category | flops | bytes accessed | tf_op | source)
XLA Modules:
  0.0 451.8 jit_solution(11851309897819754107)
XLA Ops:
  7.2 1.2 convert_reduce_fusion
  8.5 13.0 %all-reduce.1 = (f32[256]{0:T(256)S(1)}, f32[256]{0:T(256)S(1)}) all-reduce(f32[256]{0:T(256)S(1)} %get-tuple-element.119, f32[256]{0:T(256)S(1)} %get-tuple-element.118), channel_id=1, replica_groups=mesh['seq'=4,'tp'=8] {'tp'}, use_global_device_ids=true, to_apply=%region_3.0 | all-reduce | flops 512 | bytes 4096 | tf_op jit(solution)/shard_map/psum | solution.py:99
  21.5 1.7 fusion.31
  23.2 1.3 copy-done.1
  24.5 1.0 fusion.20
  25.5 6.2 %copy.30 = bf16[1280,3,512]{0,2,1:T(8,128)(2,1)} copy(bf16[1280,3,512]{2,0,1:T(8,128)(2,1)} %param.14) | data formatting | bytes 7864320 | tf_op args[4]
  31.9 0.6 copy-done.8
  32.6 0.9 fusion.30
  33.5 27.2 %all-gather.7.cloned.1.call-done = bf16[256,5120]{1,0:T(8,128)(2,1)} async-done(((bf16[256,640]{1,0:T(8,128)(2,1)}), bf16[256,5120]{1,0:T(8,128)(2,1)}) %all-gather.7.cloned.1.call-update) | async-done | bytes 2621456 | tf_op jit(solution)/shard_map/all_gather | solution.py:114
  60.7 149.2 %all-gather.9.cloned.1.call-done = bf16[5120,3,512]{0,2,1:T(8,128)(2,1)} async-done(((bf16[1280,3,512]{0,2,1:T(8,128)(2,1)}), bf16[5120,3,512]{0,2,1:T(8,128)(2,1)}) %all-gather.9.cloned.1.call-update) | async-done | bytes 15728656 | tf_op jit(solution)/shard_map/all_gather | solution.py:115
  209.8 8.5 %fusion.36 = f32[256,1536]{1,0:T(8,128)S(1)} fusion(bf16[256,5120]{1,0:T(8,128)(2,1)} %all-gather.7.cloned.1.call-done, bf16[5120,1536]{0,1:T(8,128)(2,1)} %bitcast.97), kind=kOutput, calls=%fused_computation.80 | convolution fusion | flops 4026531840 | bytes 19922944 | tf_op jit(solution)/shard_map/dot_general | solution.py:117
  218.5 12.8 %all-reduce = (f32[256]{0:T(256)S(1)}, f32[256]{0:T(256)S(1)}) all-reduce(f32[256]{0:T(256)S(1)} %get-tuple-element.117, f32[256]{0:T(256)S(1)} %get-tuple-element.116), channel_id=1, replica_groups=mesh['seq'=4,'tp'=8] {'tp'}, use_global_device_ids=true, to_apply=%region_5.0 | all-reduce | flops 512 | bytes 4096 | tf_op jit(solution)/shard_map/psum | solution.py:121
  231.7 11.3 %slice.44 = f32[256,4,64]{2,1,0:T(4,128)} slice(f32[256,4,128]{2,1,0:T(4,128)S(1)} %reshape.193), slice={[0:256:1], [0:4:1], [0:128:2]} | slice | bytes 524288 | tf_op jit(solution)/shard_map/slice | solution.py:28
  243.0 11.1 %slice.48 = f32[256,4,64]{2,1,0:T(4,128)S(1)} slice(f32[256,4,128]{2,1,0:T(4,128)S(1)} %reshape.193), slice={[0:256:1], [0:4:1], [1:128:2]} | slice | bytes 524288 | tf_op jit(solution)/shard_map/slice | solution.py:29
  254.3 11.3 %slice.50 = f32[256,4,64]{2,1,0:T(4,128)} slice(f32[256,4,128]{2,1,0:T(4,128)S(1)} %reshape.195), slice={[0:256:1], [0:4:1], [0:128:2]} | slice | bytes 524288 | tf_op jit(solution)/shard_map/slice | solution.py:28
  265.5 11.4 %slice.51 = f32[256,4,64]{2,1,0:T(4,128)} slice(f32[256,4,128]{2,1,0:T(4,128)S(1)} %reshape.195), slice={[0:256:1], [0:4:1], [1:128:2]} | slice | bytes 524288 | tf_op jit(solution)/shard_map/slice | solution.py:29
  277.4 1.2 copy.48
  278.7 0.2 copy.49
  278.9 1.1 fusion.27
  280.2 0.3 copy.33
  280.5 0.8 convert_element_type.76
  281.4 0.7 slice.80
  282.2 0.5 all-gather.15.cloned.1.call-update
  282.8 8.2 %all-gather = s32[4,1,256]{2,1,0:T(1,128)S(1)} all-gather(s32[1,1,256]{2,1,0:T(1,128)S(1)} %bitcast.93), channel_id=1, replica_groups=mesh['seq'=4,'tp'=8] {'seq'}, dimensions={0}, use_global_device_ids=true | all-gather | bytes 5120 | tf_op jit(solution)/shard_map/all_gather | solution.py:137
  291.2 0.9 copy.38
  292.1 16.6 %all-gather.11.cloned.1.call-done = bf16[1024,512]{0,1:T(8,128)(2,1)} async-done(((bf16[256,512]{0,1:T(8,128)(2,1)}), bf16[1024,512]{0,1:T(8,128)(2,1)}) %all-gather.11.cloned.1.call-update) | async-done | bytes 1048592 | tf_op jit(solution)/shard_map/all_gather | solution.py:135
  308.7 1.8 reshape.194
  310.6 0.9 copy.37
  311.5 26.2 %all-gather.13.cloned.1.call-done = bf16[1024,512]{1,0:T(8,128)(2,1)} async-done(((bf16[256,512]{1,0:T(8,128)(2,1)}), bf16[1024,512]{1,0:T(8,128)(2,1)}) %all-gather.13.cloned.1.call-update) | async-done | bytes 1048592 | tf_op jit(solution)/shard_map/all_gather | solution.py:136
  337.7 2.2 reshape.196
  339.8 11.7 %while.15 = (s32[]{:T(128)}, f32[4,256]{1,0:T(4,128)S(1)}, f32[4,256]{1,0:T(4,128)S(1)}, f32[4,256,128]{2,1,0:T(8,128)}, s32[256]{0:T(256)S(1)}, /*index=5*/s32[...) while((s32[]{:T(128)}, f32[4,256]{1,0:T(4,128)S(1)}, ...), condition=%wide.region_11.12_spmd.clone, body=%wide.region_8.11_spmd.clone.sunk | while | flops 275912704 | bytes 10288260 | solution.py:89
  340.0 1.4 fusion.50
  341.4 0.5 fusion.51
  342.0 1.2 constant_dynamic-slice_fusion.5
  343.2 1.9 fusion.53
  345.2 1.4 fusion.50
  346.7 0.5 fusion.51
  347.3 1.3 constant_dynamic-slice_fusion.5
  348.6 3.0 fusion.53
  351.5 1.2 copy.40
  352.8 48.0 %all-gather.15.cloned.1.call-done = bf16[512,5120]{1,0:T(8,128)(2,1)} async-done(((bf16[512,1280]{1,0:T(8,128)(2,1)}), bf16[512,5120]{1,0:T(8,128)(2,1)}) %all-gather.15.cloned.1.call-update) | async-done | bytes 5242896 | tf_op jit(solution)/shard_map/all_gather | solution.py:145
  400.8 4.0 convolution_convert_fusion
  404.9 2.6 copy.43
  407.5 0.9 copy-done.4
  408.4 0.8 copy.41
  409.2 32.7 %reduce-scatter.4.cloned.1.call-done = bf16[640,256]{1,0:T(8,128)(2,1)} async-done(((bf16[5120,256]{1,0:T(8,128)(2,1)}), bf16[640,256]{1,0:T(8,128)(2,1)}) %reduce-scatter.4.cloned.1.call-update) | async-done | bytes 327696
  441.9 1.2 copy.44
  443.1 1.9 fusion.22
  (57 shorter events, 2.5 us)
Async XLA Ops:
  7.2 14.3 %copy-start = (f32[4,3,640]{2,0,1:T(4,128)S(1)}, f32[4,3,640]{2,0,1:T(4,128)}, u32[]{:S(2)}) copy-start(f32[4,3,640]{2,0,1:T(4,128)} %param.13) | copy-start | bytes 92164
  7.2 17.3 %copy-start.2 = (bf16[256,640]{1,0:T(8,128)(2,1)S(1)}, bf16[256,640]{1,0:T(8,128)(2,1)}, u32[]{:S(2)}) copy-start(bf16[256,640]{1,0:T(8,128)(2,1)} %param.10) | copy-start | bytes 983044
  7.2 53.5 %all-gather.7.cloned.1.call-start = ((), (), s32[]{:S(2)}) async-start(), calls=%async_computation.1 | async-start | bytes 2949120 | tf_op jit(solution)/shard_map/all_gather | solution.py:114
  23.2 1.3 copy-start.1
  25.5 184.3 %all-gather.9.cloned.1.call-start = ((), (), s32[]{:S(2)}) async-start(), calls=%async_computation.2 | async-start | bytes 19660800 | tf_op jit(solution)/shard_map/all_gather | solution.py:115
  31.8 0.7 copy-start.8
  31.8 276.9 %all-gather.11.cloned.1.call-start = ((), (), s32[]{:S(2)}) async-start(), calls=%async_computation.3 | async-start | bytes 1310720 | tf_op jit(solution)/shard_map/all_gather | solution.py:135
  209.8 21.5 %copy-start.9 = (f32[512]{0:T(512)S(1)}, f32[512]{0:T(512)}, u32[]{:S(2)}) copy-start(f32[512]{0:T(512)} %param.15) | copy-start | bytes 6148
  209.8 21.5 %copy-start.10 = (f32[512]{0:T(512)S(1)}, f32[512]{0:T(512)}, u32[]{:S(2)}) copy-start(f32[512]{0:T(512)} %param.16) | copy-start | bytes 6148
  254.2 22.7 %copy-start.5 = (f32[256,4,64]{2,1,0:T(4,128)S(1)}, f32[256,4,64]{2,1,0:T(4,128)}, u32[]{:S(2)}) copy-start(f32[256,4,64]{2,1,0:T(4,128)} %slice.44) | copy-start | bytes 786436
  276.9 1.7 copy-start.6
  280.0 2.8 copy-start.7
  281.3 56.3 %all-gather.13.cloned.1.call-start = ((), (), s32[]{:S(2)}) async-start(), calls=%async_computation.4 | async-start | bytes 1310720 | tf_op jit(solution)/shard_map/all_gather | solution.py:136
  282.1 118.7 %all-gather.15.cloned.1.call-start = ((), (), s32[]{:S(2)}) async-start(), calls=%async_computation.5 | async-start | bytes 6553600 | tf_op jit(solution)/shard_map/all_gather | solution.py:145
  282.7 159.2 %reduce-scatter.4.cloned.1.call-start = ((), (), s32[]{:S(2)}) async-start(), calls=%async_computation.6 | async-start | bytes 2949120
  407.4 0.9 copy-start.4
  407.4 35.6 %copy-start.3 = (bf16[256,640]{1,0:T(8,128)(2,1)S(1)}, bf16[256,640]{1,0:T(8,128)(2,1)}, u32[]{:S(2)}) copy-start(bf16[256,640]{1,0:T(8,128)(2,1)} %param.10) | copy-start | bytes 983044
Sparse Core Ops, SparseCore 0:
  25.6 35.0 all-gather.6
  62.5 147.2 all-gather.8
  281.4 27.2 all-gather.10
  311.0 26.6 all-gather.12
  339.4 61.4 all-gather.14
  407.6 34.2 reduce-scatter.3
where the time goes:
time: 458 us; the launch traced here: 452 us
  waiting for transfers between devices  300 us (66%)
  local copies, waits for them, and re-layouts  72.4 us (16%)
  blocking collectives  34.1 us (7%)
  matrix products  21.9 us (5%)
  between operations  14.4 us (3%)
  other arithmetic  8.41 us (2%)
    all_gather x1, waiting for transfers between devices, body(): portion = lax.all_gather(w_qkv, 'seq', axis=0, tiled=True)  149 us
    all_gather x1, waiting for transfers between devices, body(): lax.all_gather(w_out, 'seq', axis=1, tiled=True)  48 us
    unnamed x7, waiting for transfers between devices  33.3 us
    all_gather x1, waiting for transfers between devices, body(): full_rows = lax.all_gather(modded, 'tp', axis=1, tiled=True)  27.2 us
    all_gather x1, waiting for transfers between devices, body(): value_rows = lax.all_gather(v_cache, 'seq', axis=0, tiled=True)  26.2 us
    slice x2, local copies, waits for them, and re-layouts, rotate_pairs(): even_part = field[..., 0::2]  22.6 us
    slice x2, local copies, waits for them, and re-layouts, rotate_pairs(): odd_part = field[..., 1::2]  22.5 us
    unnamed x32, local copies, waits for them, and re-layouts  17.4 us
  transfers between devices with their start and end apart: 6, of which 6 were waited for; matrix products, arithmetic and copies ran while one was open for 6% of the time, Pallas kernels for 0%

commit v1 on v0

--- a/solution.py
+++ b/solution.py
@@ -1,8 +1,12 @@
+import functools
 import math
 
 import jax
 import jax.numpy as jnp
+import numpy as np
 from jax import lax
+from jax.experimental import pallas as pl
+from jax.experimental.pallas import tpu as pltpu
 from jax.sharding import PartitionSpec as P
 
 HEAD_DIM = 128
@@ -152,6 +156,398 @@
     return (hidden_out, k_cache, v_cache)
 
 
+MESH = pl.DeviceIdType.MESH
+EXACT = lax.Precision.HIGHEST
+FAR = -1e30
+
+
+def dot00(a, b):
+    return lax.dot_general(
+        a, b, (((0,), (0,)), ((), ())), precision=EXACT, preferred_element_type=jnp.float32
+    )
+
+
+def dot11(a, b, precision=None):
+    return lax.dot_general(
+        a, b, (((1,), (1,)), ((), ())), precision=precision, preferred_element_type=jnp.float32
+    )
+
+
+def fused(
+    n_seq, n_tp, width, all_heads,
+    hid, meta, modt, freq, w, q_gain, k_gain, w_out,
+    out, k_out, v_out,
+    meta_all, st1, gathered, full, part, parts_in, st2, st3, qkv, cosine, sine,
+    q_ext, k_ext, v_all, attn, terms, pair_in, summed, moved, arrived, gate,
+    meta_s, meta_r, st1_s, st1_r, z_s, z_r, f_s, f_r, swap_s, swap_r, p_s, p_r,
+    st2_s, st2_r, st3_s, st3_r, k_s, k_r, v_s, v_r, a_s, a_r, pair_s, pair_r,
+    mv_s, mv_r, ar_s, ar_r,
+):
+    s = lax.axis_index("seq")
+    t = lax.axis_index("tp")
+    z = t // 2
+    c = t % 2
+    rows, feats = hid.shape
+    n_z = n_tp // 2
+    sibling = z * 2 + 1 - c
+
+    def copy(src, dst, send, recv, to_s, to_t):
+        return pltpu.make_async_remote_copy(
+            src_ref=src, dst_ref=dst, send_sem=send, recv_sem=recv,
+            device_id=(to_s, to_t), device_id_type=MESH,
+        )
+
+    plane = [(s + d) % n_seq for d in range(1, n_seq)]
+    column = [(t + d) % n_tp for d in range(1, n_tp)]
+    line = [(z + d) % n_z for d in range(1, n_z)]
+
+    barrier = pltpu.get_barrier_semaphore()
+    for p in plane:
+        pl.semaphore_signal(barrier, inc=1, device_id=(p, t), device_id_type=MESH)
+    for p in column:
+        pl.semaphore_signal(barrier, inc=1, device_id=(s, p), device_id_type=MESH)
+
+    x = hid[...].astype(jnp.float32)
+    row8 = lax.broadcasted_iota(jnp.int32, (8, rows), 0)
+    ones_b = jnp.ones((8, feats), jnp.bfloat16)
+    ones_f = jnp.ones((8, feats), jnp.float32)
+    st1[t] = jnp.where(row8 == 0, dot11(ones_b, hid[...]), dot11(ones_f, x * x, EXACT))
+    meta_all[s] = meta[...]
+    pl.semaphore_wait(barrier, n_seq - 1 + n_tp - 1)
+    for p in column:
+        copy(st1.at[t], st1.at[t], st1_s.at[p], st1_r.at[t], s, p).start()
+    for p in plane:
+        copy(meta_all.at[s], meta_all.at[s], meta_s.at[p], meta_r.at[s], p, t).start()
+
+    onehot = (meta[3:4, :] == row8.astype(jnp.float32)).astype(jnp.float32)
+    modulation = dot00(onehot, modt[...])
+    gate[...] = modulation[:, 2 * feats :]
+
+    for p in column:
+        copy(st1.at[p], st1.at[p], st1_s.at[p], st1_r.at[p], s, p).wait_recv()
+    totals = jnp.sum(st1[...], axis=0)
+    mean_row = totals[0:1] / width
+    scale_row = lax.rsqrt(totals[1:2] / width - mean_row * mean_row + EPSILON)
+    both = jnp.where(row8 == 0, mean_row, jnp.where(row8 == 1, scale_row, 0.0))
+    pick = lax.broadcasted_iota(jnp.int32, (8, 128), 0)
+    mean_col = dot00(both, (pick == 0).astype(jnp.float32))[:, 0:1]
+    scale_col = dot00(both, (pick == 1).astype(jnp.float32))[:, 0:1]
+    normed = (x - mean_col) * scale_col
+    modded = normed * (1.0 + modulation[:, feats : 2 * feats]) + modulation[:, :feats]
+    gathered[z] = modded.astype(jnp.bfloat16)
+
+    for p in line:
+        copy(gathered.at[z], gathered.at[z], z_s.at[p], z_r.at[z], s, p * 2 + c).start()
+
+    def pass_on(p):
+        @pl.when(p == s)
+        def _():
+            full[c, s] = gathered[p]
+
+        @pl.when(p != s)
+        def _():
+            copy(gathered.at[p], full.at[c, s], f_s.at[p], f_r.at[s], p, t).start()
+
+    pass_on(z)
+
+    for p in plane:
+        copy(meta_all.at[p], meta_all.at[p], meta_s.at[p], meta_r.at[p], p, t).wait_recv()
+    lane = lax.broadcasted_iota(jnp.int32, (rows, 128), 1)
+    even = lane % 2 == 0
+
+    def tables(j, carry):
+        block = meta_all[j]
+        angle = dot00(block, freq[...])
+        cosine[j] = jnp.cos(angle)
+        sine[j] = jnp.where(even, -1.0, 1.0) * jnp.sin(angle)
+        seg = dot00(block, (pick == 3).astype(jnp.float32))
+        same = seg == lane.astype(jnp.float32)
+        q_ext[j, :, 128:] = same.astype(jnp.float32).astype(jnp.bfloat16)
+        k_ext[j, :, 128:] = jnp.where(same | (lane >= 8), 0.0, FAR).astype(jnp.bfloat16)
+        return carry
+
+    lax.fori_loop(0, n_seq, tables, 0)
+
+    for p in line:
+        copy(gathered.at[p], gathered.at[p], z_s.at[p], z_r.at[p], s, p * 2 + c).wait_recv()
+        pass_on(p)
+
+    def project(d, carry):
+        j = (s + d) % n_seq
+
+        @pl.when(d > 0)
+        def _():
+            copy(full.at[c, j], full.at[c, j], f_s.at[j], f_r.at[j], j, t).wait_recv()
+
+        copy(full.at[c, j], full.at[c, j], swap_s.at[j], swap_r.at[j], s, sibling).start()
+        copy(full.at[1 - c, j], full.at[1 - c, j], swap_s.at[j], swap_r.at[j], s, sibling).wait_recv()
+        for h in range(n_seq):
+            cols = slice(h * 384, (h + 1) * 384)
+            acc = jnp.dot(full[0, j], w[:feats, cols], preferred_element_type=jnp.float32)
+            acc += jnp.dot(full[1, j], w[feats:, cols], preferred_element_type=jnp.float32)
+            part[j, h] = acc.astype(jnp.bfloat16)
+        for p in plane:
+            copy(part.at[j, p], parts_in.at[s, j], p_s.at[j, p], p_r.at[s, j], p, t).start()
+        return carry
+
+    lax.fori_loop(0, n_seq, project, 0)
+
+    ones_h = jnp.ones((8, 128), jnp.float32)
+    st2[s] = jnp.zeros((8, rows), jnp.float32)
+
+    def collect(d, carry):
+        j = (s + d) % n_seq
+        total = part[j, s].astype(jnp.float32)
+        for p in plane:
+            copy(part.at[j, p], parts_in.at[p, j], p_s.at[j, p], p_r.at[p, j], p, t).wait_recv()
+            total += parts_in[p, j].astype(jnp.float32)
+        qkv[j] = total
+        v_all[j] = total[:, 256:].astype(jnp.bfloat16)
+        q_sq = dot11(ones_h, total[:, :128] * total[:, :128], EXACT)
+        k_sq = dot11(ones_h, total[:, 128:256] * total[:, 128:256], EXACT)
+        st2[s] = jnp.where(row8 == 2 * j, q_sq, jnp.where(row8 == 2 * j + 1, k_sq, st2[s]))
+        return carry
+
+    lax.fori_loop(0, n_seq, collect, 0)
+
+    for p in plane:
+        copy(st2.at[s], st2.at[s], st2_s.at[p], st2_r.at[s], p, t).start()
+
+    def lanes_of(h):
+        return pl.ds(pl.multiple_of(h * 128, 128), 128)
+
+    gains = (q_gain[pl.ds(s, 1), :], k_gain[pl.ds(s, 1), :])
+
+    def rotate(j, carry):
+        for i in range(2):
+            cols = slice(i * 128, (i + 1) * 128)
+            field = qkv[j, :, cols] * gains[i]
+            swapped = jnp.where(even, pltpu.roll(field, 127, 1), pltpu.roll(field, 1, 1))
+            qkv[j, :, cols] = field * cosine[j] + swapped * sine[j]
+        return carry
+
+    for p in plane:
+        copy(st2.at[p], st2.at[p], st2_s.at[p], st2_r.at[p], p, t).wait_recv()
+    st3[t] = jnp.sum(st2[...], axis=0)
+    for p in column:
+        copy(st3.at[t], st3.at[t], st3_s.at[p], st3_r.at[t], s, p).start()
+    for p in plane:
+        copy(v_all.at[p], v_out.at[:, lanes_of(s)], v_s.at[p], v_r.at[s], p, t).start()
+    v_out[:, lanes_of(s)] = v_all[s]
+    lax.fori_loop(0, n_seq, rotate, 0)
+    for p in column:
+        copy(st3.at[p], st3.at[p], st3_s.at[p], st3_r.at[p], s, p).wait_recv()
+    norm_rows = lax.rsqrt(jnp.sum(st3[...], axis=0) / all_heads + EPSILON)
+
+    def scale_rows(j, carry):
+        q_col = dot00(norm_rows, (pick == 2 * j).astype(jnp.float32))
+        k_col = dot00(norm_rows, (pick == 2 * j + 1).astype(jnp.float32))
+        q_ext[j, :, :128] = (qkv[j, :, :128] * q_col).astype(jnp.bfloat16)
+        k_ext[j, :, :128] = (qkv[j, :, 128:256] * k_col).astype(jnp.bfloat16)
+        return carry
+
+    lax.fori_loop(0, n_seq, scale_rows, 0)
+    for p in plane:
+        copy(
+            k_ext.at[p, :, pl.ds(0, 128)], k_out.at[:, lanes_of(s)], k_s.at[p], k_r.at[s], p, t
+        ).start()
+    k_out[:, lanes_of(s)] = k_ext[s, :, :128]
+
+    score_scale = 1.0 / math.sqrt(HEAD_DIM)
+
+    def attend(j, carry):
+        keys = k_ext[...].reshape(n_seq * rows, 256)
+        values = v_all[...].reshape(n_seq * rows, 128)
+        scores = dot11(q_ext[j], keys)
+        top = jnp.max(scores, axis=1, keepdims=True)
+        weights = jnp.exp((scores - top) * score_scale)
+        denominator = jnp.sum(weights, axis=1, keepdims=True)
+        mixed = jnp.dot(weights.astype(jnp.bfloat16), values, preferred_element_type=jnp.float32)
+        attn[j, :, lanes_of(s)] = (mixed / denominator).astype(jnp.bfloat16)
+        for p in plane:
+            mine = attn.at[j, :, lanes_of(s)]
+            copy(mine, mine, a_s.at[j, p], a_r.at[j, s], p, t).start()
+        return carry
+
+    lax.fori_loop(0, n_seq, attend, 0)
+
+    def out_project(j, carry):
+        for p in plane:
+            theirs = attn.at[j, :, lanes_of(p)]
+            copy(theirs, theirs, a_s.at[j, p], a_r.at[j, p], p, t).wait_recv()
+        for i in range(2):
+            cols = slice(i * feats, (i + 1) * feats)
+            terms[j, i] = jnp.dot(
+                attn[j], w_out[:, cols], preferred_element_type=jnp.float32
+            ).astype(jnp.bfloat16)
+        copy(terms.at[j, 1 - c], pair_in.at[j], pair_s.at[j], pair_r.at[j], s, sibling).start()
+        return carry
+
+    lax.fori_loop(0, n_seq, out_project, 0)
+
+    def pair_sum(d, carry):
+        j = (s + d) % n_seq
+        copy(terms.at[j, 1 - c], pair_in.at[j], pair_s.at[j], pair_r.at[j], s, sibling).wait_recv()
+        total = (terms[j, c].astype(jnp.float32) + pair_in[j].astype(jnp.float32)).astype(jnp.bfloat16)
+        summed[j] = total
+
+        @pl.when(d == 0)
+        def _():
+            moved[s] = total
+
+        @pl.when(d > 0)
+        def _():
+            copy(summed.at[j], moved.at[s], mv_s.at[j], mv_r.at[s], j, t).start()
+
+        return carry
+
+    lax.fori_loop(0, n_seq, pair_sum, 0)
+
+    def deliver(p):
+        @pl.when(p == z)
+        def _():
+            arrived[z] = moved[p]
+
+        @pl.when(p != z)
+        def _():
+            copy(moved.at[p], arrived.at[z], ar_s.at[p], ar_r.at[z], s, p * 2 + c).start()
+
+    deliver(s)
+    for p in plane:
+        copy(moved.at[p], moved.at[p], mv_s.at[p], mv_r.at[p], p, t).wait_recv()
+        deliver(p)
+    for p in line:
+        copy(arrived.at[p], arrived.at[p], ar_s.at[p], ar_r.at[p], s, p * 2 + c).wait_recv()
+    mixed = arrived[0].astype(jnp.float32)
+    for p in range(1, n_z):
+        mixed += arrived[p].astype(jnp.float32)
+    out[...] = (hid[...].astype(jnp.float32) + gate[...] * mixed).astype(jnp.bfloat16)
+
+    for p in plane:
+        mine = k_ext.at[p, :, pl.ds(0, 128)]
+        copy(mine, k_out.at[:, lanes_of(p)], k_s.at[p], k_r.at[p], p, t).wait()
+        copy(v_all.at[p], v_out.at[:, lanes_of(p)], v_s.at[p], v_r.at[p], p, t).wait()
+        copy(meta_all.at[s], meta_all.at[s], meta_s.at[p], meta_r.at[s], p, t).wait_send()
+        copy(st2.at[s], st2.at[s], st2_s.at[p], st2_r.at[s], p, t).wait_send()
+        copy(gathered.at[p], full.at[c, s], f_s.at[p], f_r.at[s], p, t).wait_send()
+        copy(summed.at[p], moved.at[s], mv_s.at[p], mv_r.at[s], p, t).wait_send()
+    for p in column:
+        copy(st1.at[t], st1.at[t], st1_s.at[p], st1_r.at[t], s, p).wait_send()
+        copy(st3.at[t], st3.at[t], st3_s.at[p], st3_r.at[t], s, p).wait_send()
+    for p in line:
+        copy(gathered.at[z], gathered.at[z], z_s.at[p], z_r.at[z], s, p * 2 + c).wait_send()
+        copy(moved.at[p], arrived.at[z], ar_s.at[p], ar_r.at[z], s, p * 2 + c).wait_send()
+
+    def drain(j, carry):
+        copy(full.at[c, j], full.at[c, j], swap_s.at[j], swap_r.at[j], s, sibling).wait_send()
+        copy(terms.at[j, 1 - c], pair_in.at[j], pair_s.at[j], pair_r.at[j], s, sibling).wait_send()
+        for p in plane:
+            copy(part.at[j, p], parts_in.at[s, j], p_s.at[j, p], p_r.at[s, j], p, t).wait_send()
+            mine = attn.at[j, :, lanes_of(s)]
+            copy(mine, mine, a_s.at[j, p], a_r.at[j, s], p, t).wait_send()
+        return carry
+
+    lax.fori_loop(0, n_seq, drain, 0)
+
+
+def frequencies():
+    part_width = HEAD_DIM // 6
+    widths = (HEAD_DIM - 4 * part_width, 2 * part_width, 2 * part_width)
+    table = np.zeros((8, HEAD_DIM), np.float32)
+    at = 0
+    for axis_number, wide in enumerate(widths):
+        exponent = np.arange(0, wide, 2, dtype=np.float32) / np.float32(wide)
+        frequency = (1.0 / np.float32(10000.0) ** exponent).astype(np.float32)
+        table[axis_number, at : at + wide] = np.repeat(frequency, 2)
+        at += wide
+    return table
+
+
+def fused_body(hidden_in, seg_ids, positions, mod_table, w_qkv, q_gain, k_gain, w_out):
+    n_seq = lax.axis_size("seq")
+    n_tp = lax.axis_size("tp")
+    rows, feats = hidden_in.shape
+    depth, _, heads_width = w_qkv.shape
+    segs = mod_table.shape[0]
+    meta = jnp.concatenate(
+        [positions, seg_ids[None], jnp.zeros((4, rows), jnp.int32)], axis=0
+    ).astype(jnp.float32)
+    modt = jnp.pad(mod_table.reshape(segs, 3 * feats), ((0, 8 - segs), (0, 0)))
+    w = (
+        w_qkv.reshape(depth, 3, n_seq, HEAD_DIM)
+        .transpose(0, 2, 1, 3)
+        .reshape(depth, 3 * heads_width)
+    )
+    bf16, f32 = jnp.bfloat16, jnp.float32
+    n_z = n_tp // 2
+    dma = pltpu.SemaphoreType.DMA
+    scratch = [
+        pltpu.VMEM((n_seq, 8, rows), f32),
+        pltpu.VMEM((n_tp, 8, rows), f32),
+        pltpu.VMEM((n_z, rows, feats), bf16),
+        pltpu.VMEM((2, n_seq, rows, feats), bf16),
+        pltpu.VMEM((n_seq, n_seq, rows, 384), bf16),
+        pltpu.VMEM((n_seq, n_seq, rows, 384), bf16),
+        pltpu.VMEM((n_seq, 8, rows), f32),
+        pltpu.VMEM((n_tp, 8, rows), f32),
+        pltpu.VMEM((n_seq, rows, 384), f32),
+        pltpu.VMEM((n_seq, rows, 128), f32),
+        pltpu.VMEM((n_seq, rows, 128), f32),
+        pltpu.VMEM((n_seq, rows, 256), bf16),
+        pltpu.VMEM((n_seq, rows, 256), bf16),
+        pltpu.VMEM((n_seq, rows, 128), bf16),
+        pltpu.VMEM((n_seq, rows, heads_width), bf16),
+        pltpu.VMEM((n_seq, 2, rows, feats), bf16),
+        pltpu.VMEM((n_seq, rows, feats), bf16),
+        pltpu.VMEM((n_seq, rows, feats), bf16),
+        pltpu.VMEM((n_seq, rows, feats), bf16),
+        pltpu.VMEM((n_z, rows, feats), bf16),
+        pltpu.VMEM((rows, feats), f32),
+    ]
+    square = (n_seq, n_seq)
+    shapes = [
+        (n_seq,), (n_tp,), (n_z,), (n_seq,), (n_seq,), square,
+        (n_seq,), (n_tp,), (n_seq,), (n_seq,), square, (n_seq,), (n_seq,), (n_z,),
+    ]
+    for shape in shapes:
+        scratch += [dma(shape), dma(shape)]
+    vmem = pl.BlockSpec(memory_space=pltpu.VMEM)
+    return pl.pallas_call(
+        functools.partial(fused, n_seq, n_tp, feats * n_tp, heads_width * n_tp),
+        out_shape=(
+            jax.ShapeDtypeStruct((rows, feats), bf16),
+            jax.ShapeDtypeStruct((rows, heads_width), bf16),
+            jax.ShapeDtypeStruct((rows, heads_width), bf16),
+        ),
+        in_specs=[vmem] * 8,
+        out_specs=(vmem, vmem, vmem),
+        scratch_shapes=scratch,
+        compiler_params=pltpu.CompilerParams(
+            collective_id=0, has_side_effects=True, vmem_limit_bytes=58 * 1024 * 1024
+        ),
+        cost_estimate=pl.CostEstimate(
+            flops=6_000_000_000, bytes_accessed=8_000_000, transcendentals=1_200_000
+        ),
+    )(
+        hidden_in, meta, modt, jnp.asarray(frequencies()), w,
+        q_gain.reshape(n_seq, HEAD_DIM), k_gain.reshape(n_seq, HEAD_DIM), w_out,
+    )
+
+
+def pick_body(*operands):
+    hidden_in, seg_ids, positions, mod_table, w_qkv = operands[:5]
+    n_seq, n_tp = lax.axis_size("seq"), lax.axis_size("tp")
+    fits = (
+        n_tp == 2 * n_seq
+        and n_seq == 4
+        and w_qkv.shape[2] == n_seq * HEAD_DIM
+        and w_qkv.shape[0] == 2 * hidden_in.shape[1]
+        and hidden_in.shape[0] == 256
+        and mod_table.shape[0] <= 8
+    )
+    return (fused_body if fits else body)(*operands)
+
+
 def solution(mesh):
     in_specs = (
         P("seq", "tp"),
@@ -164,4 +560,4 @@
         P("tp", "seq"),
     )
     out_specs = (P("seq", "tp"), P("seq", "tp"), P("seq", "tp"))
-    return jax.shard_map(body, mesh=mesh, in_specs=in_specs, out_specs=out_specs, check_vma=False)
+    return jax.shard_map(pick_body, mesh=mesh, in_specs=in_specs, out_specs=out_specs, check_vma=False)

time: 458 us -> 190 us (0.41)
  waiting for transfers between devices: 300 us -> 0 us
  Pallas kernels: 0 us -> 163 us
  local copies, waits for them, and re-layouts: 72.4 us -> 22.5 us
  blocking collectives: 34.1 us -> 0 us
  matrix products: 21.9 us -> 0 us
  between operations: 14.4 us -> 0.65 us
  other arithmetic: 8.41 us -> 0.67 us
    all_gather x5 -> x0, waiting for transfers between devices: 267 us -> none  [the longest x1 149 us: body(): portion = lax.all_gather(w_qkv, 'seq', axis=0, tiled=True)]
    pallas_call x0 -> x1, Pallas kernels: none -> 163 us  [fused_body(): pl.pallas_call(functools.partial(fused, n_seq, n_tp, feats * n_tp, heads_...]
    slice x5 -> x0, local copies, waits for them, and re-layouts: 45.8 us -> none  [the longest x2 22.6 us: rotate_pairs(): even_part = field[..., 0::2]]
    unnamed x7 -> x0, waiting for transfers between devices: 33.3 us -> none
    psum x2 -> x0, blocking collectives: 25.8 us -> none  [the longest x1 13 us: body(): lax.psum((jnp.sum(x_float, axis=1), jnp.sum(x_float * x_float, axis=1)),...]
    dot_general x7 -> x0, matrix products: 21.9 us -> none  [the longest x1 8.5 us: body(): projected = jnp.dot(full_rows, flat, preferred_element_type=jnp.float32)]
    all_gather x1 -> x0, blocking collectives: 8.2 us -> none  [body(): seg_k = lax.all_gather(seg_ids, 'seq', axis=0, tiled=True)]
    unnamed x32 -> x10, local copies, waits for them, and re-layouts: 17.4 us -> 11.2 us
  transfers between devices with their start and end apart: 6 -> 0, of which waited for: 6 -> 0; matrix products, arithmetic and copies ran while one was open for 6% -> 0% of each run, Pallas kernels for 0% -> 0%
where the time goes in v1:
time: 190 us; the launch traced here: 187 us
  Pallas kernels  163 us (86%)
  local copies, waits for them, and re-layouts  22.5 us (12%)
    pallas_call x1, Pallas kernels, fused_body(): pl.pallas_call(functools.partial(fused, n_seq, n_tp, feats * n_tp, heads_...  163 us
    unnamed x10, local copies, waits for them, and re-layouts  11.2 us
    reshape x1, local copies, waits for them, and re-layouts, fused_body(): w = w_qkv.reshape(depth, 3, n_seq, HEAD_DIM).transpose(0, 2, 1, 3).reshap...  6.31 us
    transpose x1, local copies, waits for them, and re-layouts, fused_body(): w = w_qkv.reshape(depth, 3, n_seq, HEAD_DIM).transpose(0, 2, 1, 3).reshap...  4.29 us

profile of v1, /device:TPU:14, one launch (start us, length us, event | category | flops | bytes accessed | tf_op | source)
XLA Modules:
  0.0 187.3 jit_solution(13154819096986868780)
XLA Ops:
  0.6 6.1 %copy.15 = bf16[1280,3,512]{0,2,1:T(8,128)(2,1)} copy(bf16[1280,3,512]{2,0,1:T(8,128)(2,1)} %param.13) | data formatting | bytes 7864320 | tf_op args[4]
  6.7 4.3 %copy.16 = bf16[1280,4,3,128]{0,3,2,1:T(8,128)(2,1)} copy(bf16[1280,4,3,128]{0,3,1,2:T(8,128)(2,1)} %bitcast.9) | data formatting | bytes 7864320 | tf_op jit(solution)/shard_map/transpose | solution.py:478
  11.0 0.0 copy-start
  11.0 0.0 copy-start.1
  11.0 0.0 copy-start.2
  11.0 6.3 %copy.17.w = bf16[1280,1536]{1,0:T(8,128)(2,1)} copy(bf16[1280,1536]{0,1:T(8,128)(2,1)} %bitcast.8) | data formatting | bytes 7864320 | tf_op jit(solution)/shard_map/reshape | solution.py:479
  17.4 0.0 copy-done
  17.4 0.6 pad.4.modt
  18.0 0.1 pad.7.clone
  18.1 0.0 copy-done.1
  18.1 0.0 copy-done.2
  18.1 0.7 add_convert_fusion.meta
  18.7 163.5 %shard_map.112 = (bf16[256,640]{1,0:T(8,128)(2,1)}, bf16[256,512]{1,0:T(8,128)(2,1)}, bf16[256,512]{1,0:T(8,128)(2,1)}) custom-call(bf16[256,640]{1,0:T(8,128)(2,1)} %hid.1, f32[8,256]{1,0:T(8,128)} %add_convert_fusion.meta, f32[8,1920]{1,0:T(8,128)} %pad.4.modt, f32[8,128]{1,0:T(8,128)} %constant.7.clone.freq, bf16[1280,1536]{1,0:T(8,128)(2,1)} %copy.17.w, ...), custom_call_target="tpu_custom_call" | custom-call | flops 6000000000 | bytes 8000000 | tf_op jit(solution)/shard_map/pallas_call | solution.py:515
  182.2 1.7 copy.21
  183.9 1.7 copy.22
  185.6 1.7 copy.23
  (1 shorter events, 0.0 us)
Async XLA Ops:
  11.0 6.3 %copy-start = (f32[4,3,640]{2,0,1:T(4,128)S(1)}, f32[4,3,640]{2,0,1:T(4,128)}, u32[]{:S(2)}) copy-start(f32[4,3,640]{2,0,1:T(4,128)} %param.12) | copy-start | bytes 92164
  11.0 7.0 %copy-start.1 = (s32[3,256]{1,0:T(4,128)S(1)}, s32[3,256]{1,0:T(4,128)}, u32[]{:S(2)}) copy-start(s32[3,256]{1,0:T(4,128)} %param.11) | copy-start | bytes 9220
  11.0 7.0 %copy-start.2 = (s32[256]{0:T(256)S(1)}, s32[256]{0:T(256)}, u32[]{:S(2)}) copy-start(s32[256]{0:T(256)} %param.10) | copy-start | bytes 3076
